TPU v7x, 32 devices: a whole 2x2x4 slice. The times are simulated.
32 devices in a mesh: row: 4 (over y, x), col: 4 (over z), depth: 2 (over core).
Axes of the slice: x: 2, y: 2, z: 4, core: 2. Of those that a mesh axis runs over, the one named last changes fastest.
Arguments:
- node_features: bfloat16 [4096, 512], P(('row', 'col'), 'depth'), may hold values from -6 to 6
- weight: bfloat16 [512, 512], P('depth'), may hold values from -0.25 to 0.25
- cotangent: bfloat16 [4096, 512], P(('row', 'col'), 'depth'), may hold values from -6 to 6
- diffusion_time: float32 [1], replicated, may hold values from 0.5 to 2
- tile_count: int32 [4, 4], P('row', 'col'), may hold values from 2 to 24, as said below
- tile_row: int32 [4, 4, 24], P('row', 'col'), may hold values from 0 to 3, as said below
- tile_col: int32 [4, 4, 24], P('row', 'col'), may hold values from 0 to 3, as said below
- tile_vals: bfloat16 [4, 4, 24, 256, 256], P('row', 'col'), may hold values from -0.07782233 to 0.07782233, as said below
Outputs:
- grad_features: bfloat16 [4096, 512], P(('row', 'col'), 'depth')
- grad_weight: float32 [512, 512], P('depth')
Inputs may be any that keep to these rules, and one draw needn't show every extreme that they name: Block (r, c) uses its slots 0 to tile_count[r, c] - 1; the largest count, 24, is reached by some block in every draw. `tile_row`: tile rows index the 4 tile rows of the block's node-row range; positions may repeat. `tile_col`: tile columns index the 4 tile columns of the block; positions may repeat. `tile_vals`: edge weights, about half of them zero.
All inputs are finite; a program needn't handle non-finite values.
Results may differ from a plain program's by a relative error of at most 0.022.
Values may be sent and summed in bfloat16 or wider, within the bound.
A program may use at most 64 MiB of HBM per device.

v0:
```python
import math

import jax
import jax.numpy as jnp
from jax import lax
from jax.sharding import PartitionSpec as P


def slot_products(values, source_idx, source, transpose):
    tile_side = values.shape[-1]
    feature_width = source.shape[1]
    as_tiles = source.reshape(-1, tile_side, feature_width)
    picked = as_tiles[source_idx]
    if transpose:
        return jnp.einsum("sik,sih->skh", values, picked, preferred_element_type=jnp.float32)
    return jnp.einsum("sik,skh->sih", values, picked, preferred_element_type=jnp.float32)


def place_slots(contrib, live_slots, target_idx, first_tile, target_tiles):
    tile_side = contrib.shape[1]
    feature_width = contrib.shape[2]
    shifted = target_idx - first_tile
    inside = (shifted >= 0) & (shifted < target_tiles)
    safe_idx = jnp.where(inside, shifted, 0)
    weights = live_slots * inside.astype(jnp.float32)
    start = jnp.zeros((target_tiles, tile_side, feature_width), jnp.float32)
    summed = start.at[safe_idx].add(contrib * weights[:, None, None])
    return summed.reshape(target_tiles * tile_side, feature_width)


def per_device(
    node_features, weight, cotangent, diffusion_time, tile_count, tile_row, tile_col, tile_vals
):
    values = tile_vals[0, 0]
    tile_rows = tile_row[0, 0]
    tile_cols = tile_col[0, 0]
    slot_count = values.shape[0]
    tile_side = values.shape[-1]
    live_slots = (jnp.arange(slot_count, dtype=jnp.int32) < tile_count[0, 0]).astype(jnp.float32)
    row_devices = lax.axis_size("row")
    col_devices = lax.axis_size("col")
    piece_rows = node_features.shape[0]
    piece_tiles = piece_rows // tile_side
    row_tiles = col_devices * piece_tiles
    col_tiles = row_devices * piece_tiles
    node_total = piece_rows * row_devices * col_devices
    grad_scale = 1.0 / math.sqrt(node_total)
    elapsed = diffusion_time[0]
    damping = jnp.exp(-elapsed)
    coef_one = elapsed * damping
    coef_two = elapsed * elapsed * damping * 0.5

    def adjoint(source):
        gathered = lax.all_gather(source, "col", axis=0, tiled=True)
        contrib = slot_products(values, tile_rows, gathered, True)
        partial_value = place_slots(contrib, live_slots, tile_cols, 0, col_tiles)
        return lax.psum_scatter(
            partial_value.astype(jnp.bfloat16), "row", scatter_dimension=0, tiled=True
        ).astype(jnp.float32)

    def forward(source):
        gathered = lax.all_gather(source, "row", axis=0, tiled=True)
        contrib = slot_products(values, tile_cols, gathered, False)
        partial_value = place_slots(contrib, live_slots, tile_rows, 0, row_tiles)
        return lax.psum_scatter(
            partial_value.astype(jnp.bfloat16), "col", scatter_dimension=0, tiled=True
        ).astype(jnp.float32)

    first_hop = forward(node_features).astype(jnp.bfloat16)
    second_hop = forward(first_hop)
    diffused = (
        damping * node_features.astype(jnp.float32)
        + coef_one * first_hop.astype(jnp.float32)
        + coef_two * second_hop
    ).astype(jnp.bfloat16)
    full_cotangent = lax.all_gather(cotangent, "depth", axis=1, tiled=True)
    pulled = lax.dot_general(
        full_cotangent, weight, (((1,), (1,)), ((), ())), preferred_element_type=jnp.float32
    ).astype(jnp.bfloat16)
    back_one = adjoint(pulled).astype(jnp.bfloat16)
    back_two = adjoint(back_one)
    grad_features = (
        damping * pulled.astype(jnp.float32)
        + coef_one * back_one.astype(jnp.float32)
        + coef_two * back_two
    ).astype(jnp.bfloat16)
    partial_grad = lax.dot_general(
        diffused, full_cotangent, (((0,), (0,)), ((), ())), preferred_element_type=jnp.float32
    )
    grad_weight = lax.psum(partial_grad * grad_scale, ("row", "col"))
    return (grad_features, grad_weight)


def solution(mesh):
    return jax.shard_map(
        per_device,
        mesh=mesh,
        in_specs=(
            P(("row", "col"), "depth"),
            P("depth", None),
            P(("row", "col"), "depth"),
            P(),
            P("row", "col"),
            P("row", "col", None),
            P("row", "col", None),
            P("row", "col", None, None, None),
        ),
        out_specs=(P(("row", "col"), "depth"), P("depth", None)),
        check_vma=False,
    )
```

profile of v0, /device:TPU:0, one launch (start us, length us, event | category | flops | bytes accessed | tf_op | source)
XLA Modules:
  0.0 359.4 jit_solution(1474120210261717108)
XLA Ops:
  7.2 0.0 copy-start
  7.2 0.0 reduce-scatter.9.cloned.1.call-start
  7.2 1.3 fusion.21
  9.2 0.7 fusion.22
  9.9 13.1 %all_gather.18 = bf16[1024,256]{1,0:T(8,128)(2,1)} all-gather(bf16[256,256]{1,0:T(8,128)(2,1)} %param.8), channel_id=1, replica_groups=mesh['row'=4,'col'=4,'depth'=2] {'row'}, dimensions={0}, use_global_device_ids=true | all-gather | bytes 655360 | tf_op jit(solution)/shard_map/all_gather | solution.py:62
  23.0 0.7 bitcast_select_fusion
  23.7 0.0 copy-start.2
  23.7 3.6 gather_fusion.2
  27.2 0.0 copy-done.2
  27.2 0.0 copy-done
  27.2 5.8 %multiply_bitcast_fusion.1 = f32[24,256,256]{1,2,0:T(8,128)} fusion(f32[24]{0:T(128)S(1)} %bitcast_select_fusion, bf16[24,256,256]{2,1,0:T(8,128)(2,1)} %gather_fusion.2, bf16[1,1,24,256,256]{4,3,2,1,0:T(8,128)(2,1)S(1)} %copy-done), kind=kOutput, calls=%fused_computation.9 | convolution fusion | flops 806879232 | bytes 12583008 | tf_op jit(solution)/shard_map/sik,skh->sih/dot_general | solution.py:16
  33.0 6.6 %copy.19 = f32[24,256,256]{2,1,0:T(8,128)} copy(f32[24,256,256]{1,2,0:T(8,128)} %multiply_bitcast_fusion.1) | data formatting | bytes 12582912 | tf_op jit(solution)/shard_map/mul | solution.py:27
  39.6 1.1 broadcast.156.clone.3
  40.7 0.0 copy-start.1
  40.7 13.5 %scatter_fusion.2 = f32[4,256,256]{2,1,0:T(8,128)} fusion(f32[4,256,256]{2,1,0:T(8,128)} %broadcast.156.clone.3, s32[24]{0:T(128)S(1)} %get-tuple-element.4, f32[24,256,256]{2,1,0:T(8,128)} %copy.19), kind=kCustom, calls=%fused_computation.6 | custom fusion | flops 1572864 | bytes 18874464 | tf_op jit(solution)/shard_map/scatter-add | solution.py:27
  54.2 2.1 convert_element_type.80
  56.3 0.0 reduce-scatter.9.cloned.1.call-update
  56.3 0.0 reduce-scatter.5.cloned.1.call-start
  56.4 0.0 copy-done.1
  56.4 2.0 all_gather.15
  58.4 1.2 convolution_convert_fusion
  59.6 0.7 pad_clamp_fusion.1
  60.3 22.2 %all_gather.16 = bf16[1024,256]{1,0:T(8,128)(2,1)} all-gather(bf16[256,256]{1,0:T(8,128)(2,1)S(1)} %convolution_convert_fusion), channel_id=1, replica_groups=mesh['row'=4,'col'=4,'depth'=2] {'col'}, dimensions={0}, use_global_device_ids=true | all-gather | bytes 655360 | tf_op jit(solution)/shard_map/all_gather | solution.py:54
  82.5 3.6 gather_fusion
  86.0 0.7 bitcast_select_fusion.1
  86.7 0.0 copy-start.3
  86.7 0.5 copy-done.3
  87.2 5.8 %multiply_bitcast_fusion.3 = f32[24,256,256]{1,2,0:T(8,128)} fusion(f32[24]{0:T(128)S(1)} %bitcast_select_fusion.1, bf16[24,256,256]{2,1,0:T(8,128)(2,1)} %gather_fusion, bf16[1,1,24,256,256]{4,3,2,1,0:T(8,128)(2,1)S(1)} %copy-done), kind=kOutput, calls=%fused_computation.11 | convolution fusion | flops 806879232 | bytes 12583008 | tf_op jit(solution)/shard_map/sik,sih->skh/dot_general | solution.py:15
  93.0 6.6 %copy.15 = f32[24,256,256]{2,1,0:T(8,128)} copy(f32[24,256,256]{1,2,0:T(8,128)} %multiply_bitcast_fusion.3) | data formatting | bytes 12582912 | tf_op jit(solution)/shard_map/mul | solution.py:27
  99.6 1.1 broadcast.156.clone.1
  100.7 13.2 %scatter_fusion = f32[4,256,256]{2,1,0:T(8,128)} fusion(f32[4,256,256]{2,1,0:T(8,128)} %broadcast.156.clone.1, s32[24]{0:T(128)S(1)} %get-tuple-element.3, f32[24,256,256]{2,1,0:T(8,128)} %copy.15), kind=kCustom, calls=%fused_computation.4 | custom fusion | flops 1572864 | bytes 18874464 | tf_op jit(solution)/shard_map/scatter-add | solution.py:27
  113.9 2.1 convert_element_type.72
  116.0 0.0 reduce-scatter.5.cloned.1.call-update
  116.0 0.0 reduce-scatter.11.cloned.1.call-start
  116.1 0.0 reduce-scatter.9.cloned.1.call-done
  116.1 12.1 %all_gather.19 = bf16[1024,256]{1,0:T(8,128)(2,1)} all-gather(bf16[256,256]{1,0:T(8,128)(2,1)} %reduce-scatter.9.cloned.1.call-done), channel_id=1, replica_groups=mesh['row'=4,'col'=4,'depth'=2] {'row'}, dimensions={0}, use_global_device_ids=true | all-gather | bytes 655360 | tf_op jit(solution)/shard_map/all_gather | solution.py:62
  128.2 3.6 gather_fusion.3
  131.8 5.8 %multiply_bitcast_fusion = f32[24,256,256]{1,2,0:T(8,128)} fusion(f32[24]{0:T(128)} %copy-done.2, bf16[24,256,256]{2,1,0:T(8,128)(2,1)} %gather_fusion.3, bf16[1,1,24,256,256]{4,3,2,1,0:T(8,128)(2,1)S(1)} %copy-done), kind=kOutput, calls=%fused_computation.8 | convolution fusion | flops 806879232 | bytes 12583008 | tf_op jit(solution)/shard_map/sik,skh->sih/dot_general | solution.py:16
  137.6 6.5 %copy.21 = f32[24,256,256]{2,1,0:T(8,128)} copy(f32[24,256,256]{1,2,0:T(8,128)} %multiply_bitcast_fusion) | data formatting | bytes 12582912 | tf_op jit(solution)/shard_map/mul | solution.py:27
  144.2 1.1 broadcast.156.clone.2
  145.2 13.2 %scatter_fusion.3 = f32[4,256,256]{2,1,0:T(8,128)} fusion(f32[4,256,256]{2,1,0:T(8,128)} %broadcast.156.clone.2, s32[24]{0:T(128)S(1)} %get-tuple-element.4, f32[24,256,256]{2,1,0:T(8,128)} %copy.21), kind=kCustom, calls=%fused_computation.7 | custom fusion | flops 1572864 | bytes 18874464 | tf_op jit(solution)/shard_map/scatter-add | solution.py:27
  158.5 2.1 convert_element_type.83
  160.6 0.0 reduce-scatter.11.cloned.1.call-update
  160.6 0.0 reduce-scatter.7.cloned.1.call-start
  160.7 0.0 reduce-scatter.5.cloned.1.call-done
  160.7 21.0 %all_gather.17 = bf16[1024,256]{1,0:T(8,128)(2,1)} all-gather(bf16[256,256]{1,0:T(8,128)(2,1)} %reduce-scatter.5.cloned.1.call-done), channel_id=1, replica_groups=mesh['row'=4,'col'=4,'depth'=2] {'col'}, dimensions={0}, use_global_device_ids=true | all-gather | bytes 655360 | tf_op jit(solution)/shard_map/all_gather | solution.py:54
  181.6 0.0 copy-start.4
  181.6 3.6 gather_fusion.1
  185.2 0.0 copy-done.4
  185.2 5.8 %multiply_bitcast_fusion.2 = f32[24,256,256]{1,2,0:T(8,128)} fusion(f32[24]{0:T(128)S(1)} %copy-done.4, bf16[24,256,256]{2,1,0:T(8,128)(2,1)} %gather_fusion.1, bf16[1,1,24,256,256]{4,3,2,1,0:T(8,128)(2,1)S(1)} %copy-done), kind=kOutput, calls=%fused_computation.10 | convolution fusion | flops 806879232 | bytes 12583008 | tf_op jit(solution)/shard_map/sik,sih->skh/dot_general | solution.py:15
  191.0 6.6 %copy.17 = f32[24,256,256]{2,1,0:T(8,128)} copy(f32[24,256,256]{1,2,0:T(8,128)} %multiply_bitcast_fusion.2) | data formatting | bytes 12582912 | tf_op jit(solution)/shard_map/mul | solution.py:27
  197.6 1.1 broadcast.156.clone
  198.7 13.2 %scatter_fusion.1 = f32[4,256,256]{2,1,0:T(8,128)} fusion(f32[4,256,256]{2,1,0:T(8,128)} %broadcast.156.clone, s32[24]{0:T(128)S(1)} %get-tuple-element.3, f32[24,256,256]{2,1,0:T(8,128)} %copy.17), kind=kCustom, calls=%fused_computation.5 | custom fusion | flops 1572864 | bytes 18874464 | tf_op jit(solution)/shard_map/scatter-add | solution.py:27
  211.9 2.1 convert_element_type.75
  214.0 0.0 reduce-scatter.7.cloned.1.call-update
  214.0 0.0 all-reduce.2.cloned.1.call-start
  214.8 0.0 reduce-scatter.11.cloned.1.call-done
  214.8 2.1 convolution_multiply_fusion
  216.9 0.0 all-reduce.2.cloned.1.call-update
  216.9 20.7 %reduce-scatter.7.cloned.1.call-done = bf16[256,256]{1,0:T(8,128)(2,1)} async-done(((bf16[1024,256]{1,0:T(8,128)(2,1)}), bf16[256,256]{1,0:T(8,128)(2,1)}) %reduce-scatter.7.cloned.1.call-update) | async-done | bytes 131088 | tf_op jit(solution)/shard_map/reduce_scatter | solution.py:57
  237.6 1.7 add_convert_fusion.1
  239.3 111.7 %all-reduce.2.cloned.1.call-done = f32[256,512]{1,0:T(8,128)} async-done(((f32[256,512]{1,0:T(8,128)}), f32[256,512]{1,0:T(8,128)}) %all-reduce.2.cloned.1.call-update) | async-done | bytes 524304 | tf_op jit(solution)/shard_map/psum | solution.py:90
  351.0 1.9 copy.33
  (1 shorter events, 0.0 us)
Async XLA Ops:
  7.2 20.1 %copy-start = (bf16[1,1,24,256,256]{4,3,2,1,0:T(8,128)(2,1)S(1)}, bf16[1,1,24,256,256]{4,3,2,1,0:T(8,128)(2,1)}, u32[]{:S(2)}) copy-start(bf16[1,1,24,256,256]{4,3,2,1,0:T(8,128)(2,1)} %param.15) | copy-start | bytes 9437188
  7.2 108.9 %reduce-scatter.9.cloned.1.call-start = ((), (), s32[]{:S(2)}) async-start(), calls=%async_computation.6 | async-start | bytes 655360 | tf_op jit(solution)/shard_map/reduce_scatter | solution.py:65
  23.7 3.6 copy-start.2
  40.7 15.6 %copy-start.1 = (bf16[256,256]{1,0:T(8,128)(2,1)S(1)}, bf16[256,256]{1,0:T(8,128)(2,1)}, u32[]{:S(2)}) copy-start(bf16[256,256]{1,0:T(8,128)(2,1)} %param.10) | copy-start | bytes 393220
  56.3 104.3 %reduce-scatter.5.cloned.1.call-start = ((), (), s32[]{:S(2)}) async-start(), calls=%async_computation.4 | async-start | bytes 655360 | tf_op jit(solution)/shard_map/reduce_scatter | solution.py:57
  86.7 0.5 copy-start.3
  116.0 98.8 %reduce-scatter.11.cloned.1.call-start = ((), (), s32[]{:S(2)}) async-start(), calls=%async_computation.7 | async-start | bytes 655360 | tf_op jit(solution)/shard_map/reduce_scatter | solution.py:65
  160.6 77.0 %reduce-scatter.7.cloned.1.call-start = ((), (), s32[]{:S(2)}) async-start(), calls=%async_computation.5 | async-start | bytes 655360 | tf_op jit(solution)/shard_map/reduce_scatter | solution.py:57
  181.6 3.6 copy-start.4
  214.0 137.0 %all-reduce.2.cloned.1.call-start = ((), (), s32[]{:S(2)}) async-start(), calls=%async_computation.8 | async-start | bytes 1048576 | tf_op jit(solution)/shard_map/psum | solution.py:90
Sparse Core Ops, SparseCore 0:
  56.5 25.8 reduce-scatter.8
  116.1 24.3 reduce-scatter.4
  160.7 23.4 reduce-scatter.10
  214.1 23.4 reduce-scatter.6
  242.6 108.3 all-reduce.1
where the time goes:
time: 361 us; the launch traced here: 359 us
  waiting for transfers between devices  133 us (37%)
  blocking collectives  70.4 us (20%)
  other arithmetic  67.1 us (19%)
  local copies, waits for them, and re-layouts  47.4 us (13%)
  matrix products  26.6 us (7%)
  between operations  15.2 us (4%)
    psum x1, waiting for transfers between devices, per_device(): grad_weight = lax.psum(partial_grad * grad_scale, ('row', 'col'))  112 us
    scatter-add x4, other arithmetic, place_slots(): summed = start.at[safe_idx].add(contrib * weights[:, None, None])  53.1 us
    all_gather x2, blocking collectives, adjoint(): gathered = lax.all_gather(source, 'col', axis=0, tiled=True)  43.2 us
    mul x4, local copies, waits for them, and re-layouts, place_slots(): summed = start.at[safe_idx].add(contrib * weights[:, None, None])  26.3 us
    all_gather x2, blocking collectives, forward(): gathered = lax.all_gather(source, 'row', axis=0, tiled=True)  25.3 us
    reduce_scatter x2, waiting for transfers between devices, adjoint(): lax.psum_scatter(partial_value.astype(jnp.bfloat16), 'row', scatter_dimen...  20.7 us
    gather x4, local copies, waits for them, and re-layouts, slot_products(): picked = as_tiles[source_idx]  14.3 us
    dot_general x2, matrix products, slot_products(): jnp.einsum('sik,skh->sih', values, picked, preferred_element_type=jnp.flo...  11.7 us
  transfers between devices with their start and end apart: 5, of which 2 were waited for; matrix products, arithmetic and copies ran while one was open for 29% of the time, Pallas kernels for 0%

commit v1 on v0

v1 whole, which is shorter than its diff:
```python
import functools
import math

import jax
import jax.numpy as jnp
from jax import lax
from jax.experimental import pallas as pl
from jax.experimental.pallas import tpu as pltpu
from jax.sharding import PartitionSpec as P

MESH = pl.DeviceIdType.MESH
CHUNKS = 2
F32 = jnp.float32
BF16 = jnp.bfloat16


def build_block(col_tiles, count_ref, rows_ref, cols_ref, vals_ref, a_ref, filled, listed):
    slots, side = vals_ref.shape[0], vals_ref.shape[1]
    places = a_ref.shape[0]
    band = 64

    def clear(p, carry):
        filled[p] = 0
        return carry

    lax.fori_loop(0, places, clear, 0)

    def enter(s, carry):
        place = rows_ref[s] * col_tiles + cols_ref[s]
        at = filled[place]
        listed[place * slots + at] = s
        filled[place] = at + 1
        return carry

    lax.fori_loop(0, jnp.minimum(count_ref[0], slots), enter, 0)

    def add_up(p, carry):
        for b in range(side // band):
            part = pl.ds(b * band, band)

            def more(k, total):
                return total + vals_ref[listed[p * slots + k], part, :].astype(F32)

            total = lax.fori_loop(0, filled[p], more, jnp.zeros((band, side), F32))
            a_ref[p, part, :] = total.astype(BF16)
        return carry

    lax.fori_loop(0, places, add_up, 0)


def hops(
    nrow, ncol, grad_scale,
    t_ref, x_ref, w_ref, g_ref, a_hbm, gf_ref, gw_ref,
    a_ref, xt, source, part, got, own, h_all, gw_part, gw_got, gw_col, gw_sum,
    a_sem, g_s, g_r, p_s, p_r, d_s, d_r, w1_s, w1_r, w2_s, w2_r, w3_s, w3_r,
):
    row, col, depth = lax.axis_index("row"), lax.axis_index("col"), lax.axis_index("depth")
    side = g_ref.shape[0]
    wide = source.shape[3]

    load_a = pltpu.make_async_copy(a_hbm, a_ref, a_sem)
    load_a.start()

    barrier = pltpu.get_barrier_semaphore()
    for i in range(1, nrow):
        pl.semaphore_signal(
            barrier, inc=1, device_id={"row": lax.rem(row + i, nrow)}, device_id_type=MESH)
    for i in range(1, ncol):
        pl.semaphore_signal(
            barrier, inc=1, device_id={"col": lax.rem(col + i, ncol)}, device_id_type=MESH)
    pl.semaphore_signal(barrier, inc=1, device_id={"depth": 1 - depth}, device_id_type=MESH)

    elapsed = t_ref[0]
    damping = jnp.exp(jnp.full((1, side), -elapsed, F32))
    coef_one = elapsed * damping
    coef_two = elapsed * elapsed * damping * 0.5

    flipped = g_ref[...].astype(F32).T.astype(BF16)
    for k in range(CHUNKS):
        source[0, k, col] = flipped[k * wide:(k + 1) * wide, :]
    pl.semaphore_wait(barrier, nrow + ncol - 1)

    def to_col(ref, dst, send, recv, i):
        return pltpu.make_async_remote_copy(
            src_ref=ref, dst_ref=dst, send_sem=send, recv_sem=recv,
            device_id={"col": lax.rem(col + i, ncol)}, device_id_type=MESH)

    def to_row(ref, dst, send, recv, i):
        return pltpu.make_async_remote_copy(
            src_ref=ref, dst_ref=dst, send_sem=send, recv_sem=recv,
            device_id={"row": lax.rem(row + i, nrow)}, device_id_type=MESH)

    def spread(hop, k, i):
        piece = source.at[hop, k, col]
        return to_col(piece, piece, g_s.at[hop, k, i], g_r.at[hop, k, i], i)

    def partial(hop, k, i):
        return to_row(
            part.at[hop, k, lax.rem(row + i, nrow)], got.at[hop, k, row],
            p_s.at[hop, k, i], p_r.at[hop, k, i], i)

    def swap(k):
        piece = h_all.at[k, depth]
        return pltpu.make_async_remote_copy(
            src_ref=piece, dst_ref=piece, send_sem=d_s.at[k], recv_sem=d_r.at[k],
            device_id={"depth": 1 - depth}, device_id_type=MESH)

    def gw_rows(k, i):
        return to_row(
            gw_part.at[k, lax.rem(row + i, nrow)], gw_got.at[k, row],
            w1_s.at[k, i], w1_r.at[k, i], i)

    def gw_cols(k, i):
        piece = gw_col.at[k, col]
        return to_col(piece, piece, w2_s.at[k, i], w2_r.at[k, i], i)

    def gw_back(k, i):
        piece = gw_sum.at[k, row]
        return to_row(piece, piece, w3_s.at[k, i], w3_r.at[k, i], i)

    def start_all(copy, n):
        for i in range(1, n):
            copy(i).start()

    def recv_all(copy, n):
        for i in range(1, n):
            copy(i).wait_recv()

    def multiply(hop, k):
        recv_all(functools.partial(spread, hop, k), ncol)

        def target(i, carry):
            goal = lax.rem(row + i, nrow)
            total = jnp.zeros((wide, side), F32)
            for j in range(ncol):
                total += jnp.dot(
                    source[hop, k, j], a_ref[j * nrow + goal], preferred_element_type=F32)

            @pl.when(i < nrow)
            def _():
                part[hop, k, goal] = total.astype(BF16)
                partial(hop, k, i).start()

            @pl.when(i == nrow)
            def _():
                own[k] = total
            return carry

        lax.fori_loop(1, nrow + 1, target, 0)

    def collect(hop, k):
        recv_all(functools.partial(partial, hop, k), nrow)
        total = own[k]
        for i in range(1, nrow):
            total += got[hop, k, lax.rem(row + i, nrow)].astype(F32)
        return total

    for k in range(CHUNKS):
        start_all(functools.partial(spread, 0, k), ncol)
    xt[...] = x_ref[...].astype(F32).T.astype(BF16)
    load_a.wait()
    for k in range(CHUNKS):
        multiply(0, k)
    for k in range(CHUNKS):
        source[1, k, col] = collect(0, k).astype(BF16)
        start_all(functools.partial(spread, 1, k), ncol)
    for k in range(CHUNKS):
        multiply(1, k)
    for k in range(CHUNKS):
        total = (
            damping * source[0, k, col].astype(F32)
            + coef_one * source[1, k, col].astype(F32)
            + coef_two * collect(1, k))
        h_all[k, depth] = total.T.astype(BF16)
        swap(k).start()
    grad = jnp.zeros((side, side), F32)
    for k in range(CHUNKS):
        swap(k).wait_recv()
        for d in range(2):
            terms = jnp.dot(xt[...], h_all[k, d], preferred_element_type=F32) * grad_scale
            gw_part[k, :, :, d * wide:(d + 1) * wide] = terms.astype(BF16).reshape(
                nrow, side // nrow, wide)
        start_all(functools.partial(gw_rows, k), nrow)
    for k in range(CHUNKS):
        for d in range(2):
            at = (d * CHUNKS + k) * wide
            grad += lax.dot_general(
                h_all[k, d], w_ref[:, at:at + wide], (((1,), (1,)), ((), ())),
                preferred_element_type=F32)
    gf_ref[...] = grad.astype(BF16)
    for k in range(CHUNKS):
        recv_all(functools.partial(gw_rows, k), nrow)
        total = gw_part[k, row].astype(F32)
        for i in range(1, nrow):
            total += gw_got[k, lax.rem(row + i, nrow)].astype(F32)
        gw_col[k, col] = total.astype(BF16)
        start_all(functools.partial(gw_cols, k), ncol)
    for k in range(CHUNKS):
        recv_all(functools.partial(gw_cols, k), ncol)
        total = gw_col[k, 0].astype(F32)
        for j in range(1, ncol):
            total += gw_col[k, j].astype(F32)
        gw_sum[k, row] = total.astype(BF16)
        start_all(functools.partial(gw_back, k), nrow)
    for k in range(CHUNKS):
        recv_all(functools.partial(gw_back, k), nrow)
        for d in range(2):
            at = (d * CHUNKS + k) * wide
            gw_ref[:, at:at + wide] = gw_sum[k, :, :, d * wide:(d + 1) * wide].reshape(side, wide)

    for k in range(CHUNKS):
        for hop in range(2):
            for i in range(1, ncol):
                spread(hop, k, i).wait_send()
            for i in range(1, nrow):
                partial(hop, k, i).wait_send()
        swap(k).wait_send()
        for i in range(1, nrow):
            gw_rows(k, i).wait_send()
            gw_back(k, i).wait_send()
        for i in range(1, ncol):
            gw_cols(k, i).wait_send()


def per_device(
    node_features, weight, cotangent, diffusion_time, tile_count, tile_row, tile_col, tile_vals
):
    nrow, ncol = lax.axis_size("row"), lax.axis_size("col")
    values = tile_vals[0, 0]
    slots, side = values.shape[0], values.shape[-1]
    features = weight.shape[1]
    half = cotangent.shape[1]
    wide = half // CHUNKS
    places = nrow * ncol
    vmem = pl.BlockSpec(memory_space=pltpu.VMEM)
    smem = pl.BlockSpec(memory_space=pltpu.SMEM)

    block = pl.pallas_call(
        functools.partial(build_block, nrow),
        out_shape=jax.ShapeDtypeStruct((places, side, side), BF16),
        in_specs=[smem, smem, smem, vmem],
        out_specs=vmem,
        scratch_shapes=[
            pltpu.SMEM((places,), jnp.int32),
            pltpu.SMEM((places * slots,), jnp.int32),
        ],
        compiler_params=pltpu.CompilerParams(vmem_limit_bytes=32 << 20),
    )(tile_count.reshape(1), tile_row.reshape(slots), tile_col.reshape(slots), values)

    dma = pltpu.SemaphoreType.DMA
    grad_features, grad_weight = pl.pallas_call(
        functools.partial(hops, nrow, ncol, 1.0 / math.sqrt(side * places)),
        out_shape=(
            jax.ShapeDtypeStruct((side, half), BF16),
            jax.ShapeDtypeStruct((half, features), BF16),
        ),
        in_specs=[smem, vmem, vmem, vmem, pl.BlockSpec(memory_space=pl.ANY)],
        out_specs=(vmem, vmem),
        scratch_shapes=[
            pltpu.VMEM((places, side, side), BF16),
            pltpu.VMEM((half, side), BF16),
            pltpu.VMEM((2, CHUNKS, ncol, wide, side), BF16),
            pltpu.VMEM((2, CHUNKS, nrow, wide, side), BF16),
            pltpu.VMEM((2, CHUNKS, nrow, wide, side), BF16),
            pltpu.VMEM((CHUNKS, wide, side), F32),
            pltpu.VMEM((CHUNKS, 2, side, wide), BF16),
            pltpu.VMEM((CHUNKS, nrow, half // nrow, 2 * wide), BF16),
            pltpu.VMEM((CHUNKS, nrow, half // nrow, 2 * wide), BF16),
            pltpu.VMEM((CHUNKS, ncol, half // nrow, 2 * wide), BF16),
            pltpu.VMEM((CHUNKS, nrow, half // nrow, 2 * wide), BF16),
            dma,
            dma((2, CHUNKS, ncol)), dma((2, CHUNKS, ncol)),
            dma((2, CHUNKS, nrow)), dma((2, CHUNKS, nrow)),
            dma((CHUNKS,)), dma((CHUNKS,)),
            dma((CHUNKS, nrow)), dma((CHUNKS, nrow)),
            dma((CHUNKS, ncol)), dma((CHUNKS, ncol)),
            dma((CHUNKS, nrow)), dma((CHUNKS, nrow)),
        ],
        compiler_params=pltpu.CompilerParams(
            collective_id=0, has_side_effects=True, vmem_limit_bytes=40 << 20),
    )(diffusion_time, node_features, weight, cotangent, block)
    return (grad_features, grad_weight.astype(F32))


def solution(mesh):
    return jax.shard_map(
        per_device,
        mesh=mesh,
        in_specs=(
            P(("row", "col"), "depth"),
            P("depth", None),
            P(("row", "col"), "depth"),
            P(),
            P("row", "col"),
            P("row", "col", None),
            P("row", "col", None),
            P("row", "col", None, None, None),
        ),
        out_specs=(P(("row", "col"), "depth"), P("depth", None)),
        check_vma=False,
    )
```

time: 361 us -> 61.8 us (0.17)
  waiting for transfers between devices: 133 us -> 0 us
  blocking collectives: 70.4 us -> 0 us
  other arithmetic: 67.1 us -> 0.85 us
  Pallas kernels: 0 us -> 54.9 us
  local copies, waits for them, and re-layouts: 47.4 us -> 3.86 us
  matrix products: 26.6 us -> 0 us
  between operations: 15.2 us -> 1.97 us
    psum x1 -> x0, waiting for transfers between devices: 112 us -> none  [per_device(): grad_weight = lax.psum(partial_grad * grad_scale, ('row', 'col'))]
    all_gather x5 -> x0, blocking collectives: 70.4 us -> none  [the longest x2 43.2 us: adjoint(): gathered = lax.all_gather(source, 'col', axis=0, tiled=True)]
    pallas_call x0 -> x2, Pallas kernels: none -> 54.9 us  [the longest x1 52.9 us: per_device(): pl.pallas_call(functools.partial(hops, nrow, ncol, 1.0 / math.sqrt(side *...]
    scatter-add x4 -> x0, other arithmetic: 53.1 us -> none  [place_slots(): summed = start.at[safe_idx].add(contrib * weights[:, None, None])]
    dot_general x6 -> x0, matrix products: 26.6 us -> none  [the longest x2 11.7 us: slot_products(): jnp.einsum('sik,skh->sih', values, picked, preferred_element_type=jnp.flo...]
    mul x4 -> x0, local copies, waits for them, and re-layouts: 26.3 us -> none  [place_slots(): summed = start.at[safe_idx].add(contrib * weights[:, None, None])]
    reduce_scatter x4 -> x0, waiting for transfers between devices: 20.8 us -> none  [the longest x2 20.7 us: adjoint(): lax.psum_scatter(partial_value.astype(jnp.bfloat16), 'row', scatter_dimen...]
    gather x4 -> x0, local copies, waits for them, and re-layouts: 14.3 us -> none  [slot_products(): picked = as_tiles[source_idx]]
  transfers between devices with their start and end apart: 5 -> 0, of which waited for: 2 -> 0; matrix products, arithmetic and copies ran while one was open for 29% -> 0% of each run, Pallas kernels for 0% -> 0%
where the time goes in v1:
time: 61.8 us; the launch traced here: 61.6 us
  Pallas kernels  54.9 us (89%)
  local copies, waits for them, and re-layouts  3.86 us (6%)
  between operations  1.97 us (3%)
  other arithmetic  0.85 us (1%)
    pallas_call x1, Pallas kernels, per_device(): pl.pallas_call(functools.partial(hops, nrow, ncol, 1.0 / math.sqrt(side *...  52.9 us
    unnamed x13, local copies, waits for them, and re-layouts  3.86 us
    pallas_call x1, Pallas kernels, per_device(): pl.pallas_call(functools.partial(build_block, nrow), out_shape=jax.ShapeD...  2.02 us

profile of v1, /device:TPU:0, one launch (start us, length us, event | category | flops | bytes accessed | tf_op | source)
XLA Modules:
  0.0 61.6 jit_solution(15917143761581434859)
XLA Ops:
  1.9 0.0 copy-start
  1.9 1.9 %copy-done = bf16[1,1,24,256,256]{4,3,2,1,0:T(8,128)(2,1)S(1)} copy-done((bf16[1,1,24,256,256]{4,3,2,1,0:T(8,128)(2,1)S(1)}, bf16[1,1,24,256,256]{4,3,2,1,0:T(8,128)(2,1)}, u32[]{:S(2)}) %copy-start) | copy-done | bytes 3145752
  3.8 0.0 copy-start.4
  3.8 0.7 %copy-done.4 = s32[1,1,24]{2,1,0:T(1,128)S(1)} copy-done((s32[1,1,24]{2,1,0:T(1,128)S(1)}, s32[1,1,24]{2,1,0:T(1,128)}, u32[]{:S(2)}) %copy-start.4) | copy-done | bytes 120
  4.5 0.0 copy-start.5
  4.5 0.7 %copy-done.5 = s32[1,1,24]{2,1,0:T(1,128)S(1)} copy-done((s32[1,1,24]{2,1,0:T(1,128)S(1)}, s32[1,1,24]{2,1,0:T(1,128)}, u32[]{:S(2)}) %copy-start.5) | copy-done | bytes 120
  5.1 0.0 copy-start.1
  5.1 0.0 copy-start.2
  5.1 0.0 copy-start.3
  5.1 2.0 %shard_map.95.a_hbm = bf16[16,256,256]{2,1,0:T(8,128)(2,1)S(1)} custom-call(s32[1]{0:T(128)} %bitcast.4.count_ref, s32[24]{0:T(128)S(1)} %bitcast.6, s32[24]{0:T(128)S(1)} %bitcast.7, bf16[24,256,256]{2,1,0:T(8,128)(2,1)S(1)} %bitcast.5), custom_call_target="tpu_custom_call" | custom-call | tf_op jit(solution)/shard_map/pallas_call | solution.py:238
  7.2 0.0 copy-done.1
  7.2 0.0 copy-done.2
  7.2 0.0 copy-done.3
  7.2 52.9 %shard_map.96 = (bf16[256,256]{1,0:T(8,128)(2,1)S(1)}, bf16[256,512]{1,0:T(8,128)(2,1)S(1)}) custom-call(f32[1]{0:T(128)S(6)} %copy.11.t_ref, bf16[256,256]{1,0:T(8,128)(2,1)S(1)} %copy-done.2, bf16[256,512]{1,0:T(8,128)(2,1)S(1)} %copy-done.1, bf16[256,256]{1,0:T(8,128)(2,1)S(1)} %copy-done.3, bf16[16,256,256]{2,1,0:T(8,128)(2,1)S(1)} %shard_map.95.a_hbm), custom_call_target="tpu_custom_call" | custom-call | tf_op jit(solution)/shard_map/pallas_call | solution.py:251
  60.0 0.9 %convert_element_type.3 = f32[256,512]{1,0:T(8,128)} convert(bf16[256,512]{1,0:T(8,128)(2,1)S(1)} %get-tuple-element.5) | non-fusion elementwise | flops 131072 | bytes 786432 | tf_op jit(solution)/shard_map/convert_element_type | solution.py:282
  60.9 0.7 %copy.13 = bf16[256,256]{1,0:T(8,128)(2,1)} copy(bf16[256,256]{1,0:T(8,128)(2,1)S(1)} %get-tuple-element.8) | data formatting | bytes 262144
Async XLA Ops:
  1.9 1.9 %copy-start = (bf16[1,1,24,256,256]{4,3,2,1,0:T(8,128)(2,1)S(1)}, bf16[1,1,24,256,256]{4,3,2,1,0:T(8,128)(2,1)}, u32[]{:S(2)}) copy-start(bf16[1,1,24,256,256]{4,3,2,1,0:T(8,128)(2,1)} %param.15) | copy-start | bytes 9437188
  3.8 0.7 %copy-start.4 = (s32[1,1,24]{2,1,0:T(1,128)S(1)}, s32[1,1,24]{2,1,0:T(1,128)}, u32[]{:S(2)}) copy-start(s32[1,1,24]{2,1,0:T(1,128)} %param.13) | copy-start | bytes 292
  4.5 0.7 %copy-start.5 = (s32[1,1,24]{2,1,0:T(1,128)S(1)}, s32[1,1,24]{2,1,0:T(1,128)}, u32[]{:S(2)}) copy-start(s32[1,1,24]{2,1,0:T(1,128)} %param.14) | copy-start | bytes 292
  5.1 2.0 %copy-start.1 = (bf16[256,512]{1,0:T(8,128)(2,1)S(1)}, bf16[256,512]{1,0:T(8,128)(2,1)}, u32[]{:S(2)}) copy-start(bf16[256,512]{1,0:T(8,128)(2,1)} %w_ref.1) | copy-start | bytes 786436
  5.1 2.0 %copy-start.2 = (bf16[256,256]{1,0:T(8,128)(2,1)S(1)}, bf16[256,256]{1,0:T(8,128)(2,1)}, u32[]{:S(2)}) copy-start(bf16[256,256]{1,0:T(8,128)(2,1)} %x_ref.1) | copy-start | bytes 393220
  5.1 2.0 %copy-start.3 = (bf16[256,256]{1,0:T(8,128)(2,1)S(1)}, bf16[256,256]{1,0:T(8,128)(2,1)}, u32[]{:S(2)}) copy-start(bf16[256,256]{1,0:T(8,128)(2,1)} %g_ref.1) | copy-start | bytes 393220

commit v2 on v1

v2 whole, which is shorter than its diff:
```python
import functools
import math

import jax
import jax.numpy as jnp
from jax import lax
from jax.experimental import pallas as pl
from jax.experimental.pallas import tpu as pltpu
from jax.sharding import PartitionSpec as P

MESH = pl.DeviceIdType.MESH
CHUNKS = 2
F32 = jnp.float32
BF16 = jnp.bfloat16


def hops(
    nrow, ncol, grad_scale,
    t_hbm, x_hbm, w_hbm, g_hbm, count_hbm, rows_hbm, cols_hbm, vals_hbm, gf_ref, gw_ref,
    t_ref, x_ref, w_ref, g_ref, count_ref, rows_ref, cols_ref, vals_ref,
    placed, rank, order, placed_at, tile_at, running, tiles,
    xt, source, total, part, got, h_all, gw_part, gw_got, gw_col, gw_back_to, gw_sum,
    load, g_s, g_r, p_s, p_r, d_s, d_r, w1_s, w1_r, w2_s, w2_r, w3_s, w3_r, w4_s, w4_r,
):
    row, col, depth = lax.axis_index("row"), lax.axis_index("col"), lax.axis_index("depth")
    side = g_ref.shape[0]
    slots = vals_ref.shape[0]
    wide = source.shape[3]
    places = nrow * ncol
    split = gw_col.shape[2] < gw_part.shape[2]

    loads = [
        pltpu.make_async_copy(src, dst, load.at[n])
        for n, (src, dst) in enumerate((
            (g_hbm, g_ref), (rows_hbm, rows_ref), (cols_hbm, cols_ref), (count_hbm, count_ref),
            (t_hbm, t_ref), (vals_hbm, vals_ref), (x_hbm, x_ref), (w_hbm, w_ref)))
    ]
    for copy in loads:
        copy.start()

    barrier = pltpu.get_barrier_semaphore()
    for i in range(1, nrow):
        pl.semaphore_signal(
            barrier, inc=1, device_id={"row": lax.rem(row + i, nrow)}, device_id_type=MESH)
    for i in range(1, ncol):
        pl.semaphore_signal(
            barrier, inc=1, device_id={"col": lax.rem(col + i, ncol)}, device_id_type=MESH)
    pl.semaphore_signal(barrier, inc=1, device_id={"depth": 1 - depth}, device_id_type=MESH)

    loads[0].wait()
    flipped = g_ref[...].astype(F32).T.astype(BF16)
    for k in range(CHUNKS):
        source[0, k, col] = flipped[k * wide:(k + 1) * wide, :]
    pl.semaphore_wait(barrier, nrow + ncol - 1)

    def to_col(ref, dst, send, recv, i):
        return pltpu.make_async_remote_copy(
            src_ref=ref, dst_ref=dst, send_sem=send, recv_sem=recv,
            device_id={"col": lax.rem(col + i, ncol)}, device_id_type=MESH)

    def to_row(ref, dst, send, recv, i):
        return pltpu.make_async_remote_copy(
            src_ref=ref, dst_ref=dst, send_sem=send, recv_sem=recv,
            device_id={"row": lax.rem(row + i, nrow)}, device_id_type=MESH)

    def pass_on(hop, k, p, up):
        piece = source.at[hop, k, p]
        return pltpu.make_async_remote_copy(
            src_ref=piece, dst_ref=piece, send_sem=g_s.at[hop, k, up, p],
            recv_sem=g_r.at[hop, k, p],
            device_id={"col": jnp.minimum(col + 1, ncol - 1) if up else jnp.maximum(col - 1, 0)},
            device_id_type=MESH)

    def partial(hop, k, i):
        return to_row(
            part.at[hop, k, lax.rem(row + i, nrow)], got.at[hop, k, row],
            p_s.at[hop, k, i], p_r.at[hop, k, i], i)

    def swap(k):
        piece = h_all.at[k, depth]
        return pltpu.make_async_remote_copy(
            src_ref=piece, dst_ref=piece, send_sem=d_s.at[k], recv_sem=d_r.at[k],
            device_id={"depth": 1 - depth}, device_id_type=MESH)

    def gw_rows(k, i):
        return to_row(
            gw_part.at[k, lax.rem(row + i, nrow)], gw_got.at[k, row],
            w1_s.at[k, i], w1_r.at[k, i], i)

    def gw_cols(k, i):
        mine = gw_back_to.at[k, lax.rem(col + i, ncol)] if split else gw_col.at[k, col]
        return to_col(mine, gw_col.at[k, col], w2_s.at[k, i], w2_r.at[k, i], i)

    def gw_share(k, i):
        piece = gw_sum.at[k, row, col]
        return to_col(piece, piece, w4_s.at[k, i], w4_r.at[k, i], i)

    def gw_back(k, i):
        piece = gw_sum.at[k, row]
        return to_row(piece, piece, w3_s.at[k, i], w3_r.at[k, i], i)

    def start_all(copy, n):
        for i in range(1, n):
            copy(i).start()

    def recv_all(copy, n):
        for i in range(1, n):
            copy(i).wait_recv()

    def spread(hop, k):
        @pl.when(col < ncol - 1)
        def _():
            pass_on(hop, k, col, 1).start()

        @pl.when(col > 0)
        def _():
            pass_on(hop, k, col, 0).start()

    def relay(hop, k, s):
        @pl.when(col >= s)
        def _():
            pass_on(hop, k, col - s, 1).wait_recv()

            @pl.when(col < ncol - 1)
            def _():
                pass_on(hop, k, col - s, 1).start()

        @pl.when(col + s < ncol)
        def _():
            pass_on(hop, k, col + s, 0).wait_recv()

            @pl.when(col > 0)
            def _():
                pass_on(hop, k, col + s, 0).start()

    def add_piece(hop, k, p, first):
        def target(goal, carry):
            term = jnp.dot(
                source[hop, k, p], tiles[tile_at[p * nrow + goal]], preferred_element_type=F32)
            if first:
                total[k, goal] = term
            else:
                total[k, goal] += term
            return carry

        lax.fori_loop(0, nrow, target, 0, unroll=nrow <= 4)

    def add_arrived(hop, k, s):
        @pl.when(col >= s)
        def _():
            add_piece(hop, k, col - s, False)

        @pl.when(col + s < ncol)
        def _():
            add_piece(hop, k, col + s, False)

    def hand_out(hop, k):
        for i in range(1, nrow):
            goal = lax.rem(row + i, nrow)
            part[hop, k, goal] = total[k, goal].astype(BF16)
            partial(hop, k, i).start()

    def collect(hop, k):
        recv_all(functools.partial(partial, hop, k), nrow)
        terms = total[k, row]
        for i in range(1, nrow):
            terms += got[hop, k, lax.rem(row + i, nrow)].astype(F32)
        return terms

    def relay_all(hop, s):
        for k in range(CHUNKS):
            relay(hop, k, s)

    for k in range(CHUNKS):
        spread(0, k)

    for copy in loads[1:4]:
        copy.wait()
    live = count_ref[0]

    def enter(s, carry):
        placed[s] = jnp.where(s < live, rows_ref[s] * nrow + cols_ref[s], places)
        return carry

    lax.fori_loop(0, slots, enter, 0)

    def count_before(s, carry):
        mine = placed[s]
        before = jnp.int32(0)
        for other in range(slots):
            theirs = placed[other]
            ahead = (theirs < mine) | ((theirs == mine) & (other < s))
            before += jnp.where(ahead, 1, 0)
        rank[s] = before
        return carry

    lax.fori_loop(0, slots, count_before, 0)

    def invert(n, carry):
        slot, place = jnp.int32(0), jnp.int32(0)
        for s in range(slots):
            here = rank[s] == n
            slot += jnp.where(here, s, 0)
            place += jnp.where(here, placed[s], 0)
        order[n] = slot
        placed_at[n] = place
        return carry

    lax.fori_loop(0, slots, invert, 0)

    def find(p, carry):
        last, held = jnp.int32(-1), jnp.int32(0)
        for s in range(slots):
            last += jnp.where(placed[s] <= p, 1, 0)
            held += jnp.where(placed[s] == p, 1, 0)
        tile_at[p] = jnp.where(held > 0, last, slots)
        return carry

    lax.fori_loop(0, places, find, 0)
    relay_all(0, 1)
    loads[5].wait()
    running[...] = jnp.zeros_like(running)
    tiles[slots] = jnp.zeros((side, side), BF16)

    def add_up(n, carry):
        slot = order[n]
        same = placed_at[n] == placed_at[jnp.maximum(n - 1, 0)]
        keep = jnp.where(same, 1.0, 0.0).astype(F32)
        for b in range(0, side, 64):
            band = pl.ds(b, 64)
            now = running[band, :] * keep + vals_ref[slot, band, :].astype(F32)
            running[band, :] = now
            tiles[n, band, :] = now.astype(BF16)
        return carry

    for s in range(1, ncol):
        if s > 1:
            relay_all(0, s)
        if s < ncol - 1:
            steps = ncol - 2
            lax.fori_loop(slots * (s - 1) // steps, slots * s // steps, add_up, 0)
    loads[6].wait()
    xt[...] = x_ref[...].astype(F32).T.astype(BF16)
    for k in range(CHUNKS):
        for s in range(ncol):
            if s == 0:
                add_piece(0, k, col, True)
            else:
                add_arrived(0, k, s)
        hand_out(0, k)
    for k in range(CHUNKS):
        source[1, k, col] = collect(0, k).astype(BF16)
        spread(1, k)
    for s in range(ncol):
        for k in range(CHUNKS):
            if s > 0:
                relay(1, k, s)
                add_arrived(1, k, s)
            else:
                add_piece(1, k, col, True)
            if s == ncol - 1:
                hand_out(1, k)

    loads[4].wait()
    elapsed = t_ref[0]
    damping = jnp.exp(jnp.full((1, side), -elapsed, F32))
    coef_one = elapsed * damping
    coef_two = elapsed * elapsed * damping * 0.5
    for k in range(CHUNKS):
        terms = (
            damping * source[0, k, col].astype(F32)
            + coef_one * source[1, k, col].astype(F32)
            + coef_two * collect(1, k))
        h_all[k, depth] = terms.T.astype(BF16)
        swap(k).start()
    loads[7].wait()
    for k in range(CHUNKS):
        swap(k).wait_recv()
        for d in range(2):
            terms = jnp.dot(xt[...], h_all[k, d], preferred_element_type=F32) * grad_scale
            gw_part[k, :, :, d * wide:(d + 1) * wide] = terms.astype(BF16).reshape(
                nrow, side // nrow, wide)
        start_all(functools.partial(gw_rows, k), nrow)
    grad = jnp.zeros((side, side), F32)
    for k in range(CHUNKS):
        for d in range(2):
            at = (d * CHUNKS + k) * wide
            grad += lax.dot_general(
                h_all[k, d], w_ref[:, at:at + wide], (((1,), (1,)), ((), ())),
                preferred_element_type=F32)
    gf_ref[...] = grad.astype(BF16)
    for k in range(CHUNKS):
        recv_all(functools.partial(gw_rows, k), nrow)
        terms = gw_part[k, row].astype(F32)
        for i in range(1, nrow):
            terms += gw_got[k, lax.rem(row + i, nrow)].astype(F32)
        if split:
            gw_back_to[k] = terms.astype(BF16).reshape(gw_back_to.shape[1:])
            gw_col[k, col] = gw_back_to[k, col]
        else:
            gw_col[k, col] = terms.astype(BF16)
        start_all(functools.partial(gw_cols, k), ncol)
    for k in range(CHUNKS):
        recv_all(functools.partial(gw_cols, k), ncol)
        terms = gw_col[k, 0].astype(F32)
        for j in range(1, ncol):
            terms += gw_col[k, j].astype(F32)
        if split:
            gw_sum[k, row, col] = terms.astype(BF16)
            start_all(functools.partial(gw_share, k), ncol)
        else:
            gw_sum[k, row, 0] = terms.astype(BF16)
            start_all(functools.partial(gw_back, k), nrow)
    if split:
        for k in range(CHUNKS):
            recv_all(functools.partial(gw_share, k), ncol)
            start_all(functools.partial(gw_back, k), nrow)
    for k in range(CHUNKS):
        recv_all(functools.partial(gw_back, k), nrow)
        for d in range(2):
            at = (d * CHUNKS + k) * wide
            gw_ref[:, at:at + wide] = gw_sum[k, :, :, :, d * wide:(d + 1) * wide].reshape(
                side, wide)

    for k in range(CHUNKS):
        for hop in range(2):
            for p in range(ncol):
                @pl.when((p <= col) & (col < ncol - 1))
                def _():
                    pass_on(hop, k, p, 1).wait_send()

                @pl.when((p >= col) & (col > 0))
                def _():
                    pass_on(hop, k, p, 0).wait_send()
            for i in range(1, nrow):
                partial(hop, k, i).wait_send()
        swap(k).wait_send()
        for i in range(1, nrow):
            gw_rows(k, i).wait_send()
            gw_back(k, i).wait_send()
        for i in range(1, ncol):
            gw_cols(k, i).wait_send()
            if split:
                gw_share(k, i).wait_send()


def per_device(
    node_features, weight, cotangent, diffusion_time, tile_count, tile_row, tile_col, tile_vals
):
    nrow, ncol = lax.axis_size("row"), lax.axis_size("col")
    values = tile_vals[0, 0]
    slots, side = values.shape[0], values.shape[-1]
    features = weight.shape[1]
    half = cotangent.shape[1]
    wide = half // CHUNKS
    places = nrow * ncol
    vmem = pl.BlockSpec(memory_space=pltpu.VMEM)

    dma = pltpu.SemaphoreType.DMA
    hbm = pl.BlockSpec(memory_space=pltpu.HBM)
    held = half // nrow
    piece = held // ncol if (held // ncol) % 16 == 0 else held
    grad_features, grad_weight = pl.pallas_call(
        functools.partial(hops, nrow, ncol, 1.0 / math.sqrt(side * places)),
        out_shape=(
            jax.ShapeDtypeStruct((side, half), BF16),
            jax.ShapeDtypeStruct((half, features), BF16),
        ),
        in_specs=[hbm] * 8,
        out_specs=(vmem, vmem),
        scratch_shapes=[
            pltpu.SMEM((1,), F32),
            pltpu.VMEM((side, half), BF16),
            pltpu.VMEM((half, features), BF16),
            pltpu.VMEM((side, half), BF16),
            pltpu.SMEM((1,), jnp.int32),
            pltpu.SMEM((slots,), jnp.int32),
            pltpu.SMEM((slots,), jnp.int32),
            pltpu.VMEM((slots, side, side), BF16),
            pltpu.SMEM((slots,), jnp.int32),
            pltpu.SMEM((slots,), jnp.int32),
            pltpu.SMEM((slots,), jnp.int32),
            pltpu.SMEM((slots,), jnp.int32),
            pltpu.SMEM((places,), jnp.int32),
            pltpu.VMEM((side, side), F32),
            pltpu.VMEM((slots + 1, side, side), BF16),
            pltpu.VMEM((half, side), BF16),
            pltpu.VMEM((2, CHUNKS, ncol, wide, side), BF16),
            pltpu.VMEM((CHUNKS, nrow, wide, side), F32),
            pltpu.VMEM((2, CHUNKS, nrow, wide, side), BF16),
            pltpu.VMEM((2, CHUNKS, nrow, wide, side), BF16),
            pltpu.VMEM((CHUNKS, 2, side, wide), BF16),
            pltpu.VMEM((CHUNKS, nrow, held, 2 * wide), BF16),
            pltpu.VMEM((CHUNKS, nrow, held, 2 * wide), BF16),
            pltpu.VMEM((CHUNKS, ncol, piece, 2 * wide), BF16),
            pltpu.VMEM((CHUNKS, held // piece, piece, 2 * wide), BF16),
            pltpu.VMEM((CHUNKS, nrow, held // piece, piece, 2 * wide), BF16),
            dma((8,)),
            dma((2, CHUNKS, 2, ncol)), dma((2, CHUNKS, ncol)),
            dma((2, CHUNKS, nrow)), dma((2, CHUNKS, nrow)),
            dma((CHUNKS,)), dma((CHUNKS,)),
            dma((CHUNKS, nrow)), dma((CHUNKS, nrow)),
            dma((CHUNKS, ncol)), dma((CHUNKS, ncol)),
            dma((CHUNKS, nrow)), dma((CHUNKS, nrow)),
            dma((CHUNKS, ncol)), dma((CHUNKS, ncol)),
        ],
        compiler_params=pltpu.CompilerParams(
            collective_id=0, has_side_effects=True, vmem_limit_bytes=56 << 20),
    )(
        diffusion_time, node_features, weight, cotangent, tile_count.reshape(1),
        tile_row.reshape(slots), tile_col.reshape(slots), values)
    return (grad_features, grad_weight.astype(F32))


def solution(mesh):
    return jax.shard_map(
        per_device,
        mesh=mesh,
        in_specs=(
            P(("row", "col"), "depth"),
            P("depth", None),
            P(("row", "col"), "depth"),
            P(),
            P("row", "col"),
            P("row", "col", None),
            P("row", "col", None),
            P("row", "col", None, None, None),
        ),
        out_specs=(P(("row", "col"), "depth"), P("depth", None)),
        check_vma=False,
    )
```

time: 61.8 us -> 61.9 us (level)
  local copies, waits for them, and re-layouts: 3.86 us -> 1.57 us
  Pallas kernels: 54.9 us -> 56.4 us
  other arithmetic: 0.85 us -> 1.8 us
    pallas_call x1, Pallas kernels: 52.9 us -> 56.4 us  [per_device(): pl.pallas_call(functools.partial(hops, nrow, ncol, 1.0 / math.sqrt(side *...]
    unnamed x13 -> x1, local copies, waits for them, and re-layouts: 3.86 us -> 1.57 us
    pallas_call x1 -> x0, Pallas kernels: 2.02 us -> none  [per_device(): pl.pallas_call(functools.partial(build_block, nrow), out_shape=jax.ShapeD...]
    convert_element_type x1, other arithmetic: 0.85 us -> 1.8 us  [per_device(): return (grad_features, grad_weight.astype(F32))]
where the time goes in v2:
time: 61.9 us; the launch traced here: 61.7 us
  Pallas kernels  56.4 us (91%)
  between operations  1.93 us (3%)
  other arithmetic  1.8 us (3%)
  local copies, waits for them, and re-layouts  1.57 us (3%)
    pallas_call x1, Pallas kernels, per_device(): pl.pallas_call(functools.partial(hops, nrow, ncol, 1.0 / math.sqrt(side *...  56.4 us
    convert_element_type x1, other arithmetic, per_device(): return (grad_features, grad_weight.astype(F32))  1.8 us
    unnamed x1, local copies, waits for them, and re-layouts  1.57 us

profile of v2, /device:TPU:0, one launch (start us, length us, event | category | flops | bytes accessed | tf_op | source)
XLA Modules:
  0.0 61.7 jit_solution(7655188378465242209)
XLA Ops:
  1.9 56.4 %shard_map.95 = (bf16[256,256]{1,0:T(8,128)(2,1)}, bf16[256,512]{1,0:T(8,128)(2,1)}) custom-call(f32[1]{0:T(128)S(6)} %copy.11.t_hbm, bf16[256,256]{1,0:T(8,128)(2,1)} %x_hbm.1, bf16[256,512]{1,0:T(8,128)(2,1)} %w_hbm.1, bf16[256,256]{1,0:T(8,128)(2,1)} %g_hbm.1, s32[1]{0:T(128)} %bitcast.4.count_hbm, s32[24]{0:T(128)} %bitcast.6, s32[24]{0:T(128)} %bitcast.7, ...), custom_call_target="tpu_custom_call" | custom-call | tf_op jit(solution)/shard_map/pallas_call | solution.py:363
  58.3 1.8 %convert_element_type.3 = f32[256,512]{1,0:T(8,128)} convert(bf16[256,512]{1,0:T(8,128)(2,1)} %get-tuple-element.5) | non-fusion elementwise | flops 131072 | bytes 786432 | tf_op jit(solution)/shard_map/convert_element_type | solution.py:412
  60.1 1.6 %copy.13 = bf16[256,256]{1,0:T(8,128)(2,1)} copy(bf16[256,256]{1,0:T(8,128)(2,1)} %get-tuple-element.8) | data formatting | bytes 262144

commit v3 on v2

--- a/solution.py
+++ b/solution.py
@@ -63,13 +63,9 @@
             src_ref=ref, dst_ref=dst, send_sem=send, recv_sem=recv,
             device_id={"row": lax.rem(row + i, nrow)}, device_id_type=MESH)
 
-    def pass_on(hop, k, p, up):
-        piece = source.at[hop, k, p]
-        return pltpu.make_async_remote_copy(
-            src_ref=piece, dst_ref=piece, send_sem=g_s.at[hop, k, up, p],
-            recv_sem=g_r.at[hop, k, p],
-            device_id={"col": jnp.minimum(col + 1, ncol - 1) if up else jnp.maximum(col - 1, 0)},
-            device_id_type=MESH)
+    def spread(hop, k, i):
+        piece = source.at[hop, k, col]
+        return to_col(piece, piece, g_s.at[hop, k, i], g_r.at[hop, k, i], i)
 
     def partial(hop, k, i):
         return to_row(
@@ -107,72 +103,46 @@
         for i in range(1, n):
             copy(i).wait_recv()
 
-    def spread(hop, k):
-        @pl.when(col < ncol - 1)
-        def _():
-            pass_on(hop, k, col, 1).start()
-
-        @pl.when(col > 0)
-        def _():
-            pass_on(hop, k, col, 0).start()
-
-    def relay(hop, k, s):
-        @pl.when(col >= s)
-        def _():
-            pass_on(hop, k, col - s, 1).wait_recv()
-
-            @pl.when(col < ncol - 1)
+    def sent_all(copy, n):
+        for i in range(1, n):
+            copy(i).wait_send()
+
+    def multiply(hop, k):
+        recv_all(functools.partial(spread, hop, k), ncol)
+
+        def target(i, carry):
+            goal = lax.rem(row + i, nrow)
+            terms = jnp.zeros((wide, side), F32)
+            for p in range(ncol):
+                terms += jnp.dot(
+                    source[hop, k, p], tiles[tile_at[p * nrow + goal]],
+                    preferred_element_type=F32)
+
+            @pl.when(i < nrow)
             def _():
-                pass_on(hop, k, col - s, 1).start()
-
-        @pl.when(col + s < ncol)
-        def _():
-            pass_on(hop, k, col + s, 0).wait_recv()
-
-            @pl.when(col > 0)
+                part[hop, k, goal] = terms.astype(BF16)
+                partial(hop, k, i).start()
+
+            @pl.when(i == nrow)
             def _():
-                pass_on(hop, k, col + s, 0).start()
-
-    def add_piece(hop, k, p, first):
-        def target(goal, carry):
-            term = jnp.dot(
-                source[hop, k, p], tiles[tile_at[p * nrow + goal]], preferred_element_type=F32)
-            if first:
-                total[k, goal] = term
-            else:
-                total[k, goal] += term
+                total[k] = terms
             return carry
 
-        lax.fori_loop(0, nrow, target, 0, unroll=nrow <= 4)
-
-    def add_arrived(hop, k, s):
-        @pl.when(col >= s)
-        def _():
-            add_piece(hop, k, col - s, False)
-
-        @pl.when(col + s < ncol)
-        def _():
-            add_piece(hop, k, col + s, False)
-
-    def hand_out(hop, k):
-        for i in range(1, nrow):
-            goal = lax.rem(row + i, nrow)
-            part[hop, k, goal] = total[k, goal].astype(BF16)
-            partial(hop, k, i).start()
+        lax.fori_loop(1, nrow + 1, target, 0)
 
     def collect(hop, k):
         recv_all(functools.partial(partial, hop, k), nrow)
-        terms = total[k, row]
+        terms = total[k]
         for i in range(1, nrow):
             terms += got[hop, k, lax.rem(row + i, nrow)].astype(F32)
         return terms
 
-    def relay_all(hop, s):
-        for k in range(CHUNKS):
-            relay(hop, k, s)
-
-    for k in range(CHUNKS):
-        spread(0, k)
+    def spread_all(hop, k):
+        if k > 0:
+            sent_all(functools.partial(spread, hop, k - 1), ncol)
+        start_all(functools.partial(spread, hop, k), ncol)
+
+    spread_all(0, 0)
 
     for copy in loads[1:4]:
         copy.wait()
@@ -217,7 +187,6 @@
         return carry
 
     lax.fori_loop(0, places, find, 0)
-    relay_all(0, 1)
     loads[5].wait()
     running[...] = jnp.zeros_like(running)
     tiles[slots] = jnp.zeros((side, side), BF16)
@@ -233,63 +202,39 @@
             tiles[n, band, :] = now.astype(BF16)
         return carry
 
-    for s in range(1, ncol):
-        if s > 1:
-            relay_all(0, s)
-        if s < ncol - 1:
-            steps = ncol - 2
-            lax.fori_loop(slots * (s - 1) // steps, slots * s // steps, add_up, 0)
-    loads[6].wait()
+    lax.fori_loop(0, slots // 2, add_up, 0)
+    for k in range(1, CHUNKS):
+        spread_all(0, k)
+    lax.fori_loop(slots // 2, slots, add_up, 0)
+    for copy in loads[4:5] + loads[6:]:
+        copy.wait()
     xt[...] = x_ref[...].astype(F32).T.astype(BF16)
-    for k in range(CHUNKS):
-        for s in range(ncol):
-            if s == 0:
-                add_piece(0, k, col, True)
-            else:
-                add_arrived(0, k, s)
-        hand_out(0, k)
-    for k in range(CHUNKS):
-        source[1, k, col] = collect(0, k).astype(BF16)
-        spread(1, k)
-    for s in range(ncol):
-        for k in range(CHUNKS):
-            if s > 0:
-                relay(1, k, s)
-                add_arrived(1, k, s)
-            else:
-                add_piece(1, k, col, True)
-            if s == ncol - 1:
-                hand_out(1, k)
-
-    loads[4].wait()
     elapsed = t_ref[0]
     damping = jnp.exp(jnp.full((1, side), -elapsed, F32))
     coef_one = elapsed * damping
     coef_two = elapsed * elapsed * damping * 0.5
-    for k in range(CHUNKS):
+
+    def turn(k):
+        source[1, k, col] = collect(0, k).astype(BF16)
+        spread_all(1, k)
+
+    def join(k):
         terms = (
             damping * source[0, k, col].astype(F32)
             + coef_one * source[1, k, col].astype(F32)
             + coef_two * collect(1, k))
         h_all[k, depth] = terms.T.astype(BF16)
         swap(k).start()
-    loads[7].wait()
-    for k in range(CHUNKS):
+
+    def gw_begin(k):
         swap(k).wait_recv()
         for d in range(2):
             terms = jnp.dot(xt[...], h_all[k, d], preferred_element_type=F32) * grad_scale
             gw_part[k, :, :, d * wide:(d + 1) * wide] = terms.astype(BF16).reshape(
                 nrow, side // nrow, wide)
         start_all(functools.partial(gw_rows, k), nrow)
-    grad = jnp.zeros((side, side), F32)
-    for k in range(CHUNKS):
-        for d in range(2):
-            at = (d * CHUNKS + k) * wide
-            grad += lax.dot_general(
-                h_all[k, d], w_ref[:, at:at + wide], (((1,), (1,)), ((), ())),
-                preferred_element_type=F32)
-    gf_ref[...] = grad.astype(BF16)
-    for k in range(CHUNKS):
+
+    def gw_over_rows(k):
         recv_all(functools.partial(gw_rows, k), nrow)
         terms = gw_part[k, row].astype(F32)
         for i in range(1, nrow):
@@ -300,7 +245,8 @@
         else:
             gw_col[k, col] = terms.astype(BF16)
         start_all(functools.partial(gw_cols, k), ncol)
-    for k in range(CHUNKS):
+
+    def gw_over_cols(k):
         recv_all(functools.partial(gw_cols, k), ncol)
         terms = gw_col[k, 0].astype(F32)
         for j in range(1, ncol):
@@ -310,30 +256,51 @@
             start_all(functools.partial(gw_share, k), ncol)
         else:
             gw_sum[k, row, 0] = terms.astype(BF16)
-            start_all(functools.partial(gw_back, k), nrow)
-    if split:
-        for k in range(CHUNKS):
+
+    def gw_return(k):
+        if split:
             recv_all(functools.partial(gw_share, k), ncol)
-            start_all(functools.partial(gw_back, k), nrow)
-    for k in range(CHUNKS):
+        start_all(functools.partial(gw_back, k), nrow)
+
+    def gw_end(k):
         recv_all(functools.partial(gw_back, k), nrow)
         for d in range(2):
             at = (d * CHUNKS + k) * wide
             gw_ref[:, at:at + wide] = gw_sum[k, :, :, :, d * wide:(d + 1) * wide].reshape(
                 side, wide)
 
+    multiply(0, 0)
+    turn(0)
+    multiply(0, 1)
+    turn(1)
+    multiply(1, 0)
+    join(0)
+    multiply(1, 1)
+    gw_begin(0)
+    join(1)
+    gw_over_rows(0)
+    gw_begin(1)
+    grad = jnp.zeros((side, side), F32)
+    for k in range(CHUNKS):
+        for d in range(2):
+            at = (d * CHUNKS + k) * wide
+            grad += lax.dot_general(
+                h_all[k, d], w_ref[:, at:at + wide], (((1,), (1,)), ((), ())),
+                preferred_element_type=F32)
+    gf_ref[...] = grad.astype(BF16)
+    gw_over_cols(0)
+    gw_over_rows(1)
+    gw_return(0)
+    gw_over_cols(1)
+    gw_return(1)
+    for k in range(CHUNKS):
+        gw_end(k)
+
     for k in range(CHUNKS):
         for hop in range(2):
-            for p in range(ncol):
-                @pl.when((p <= col) & (col < ncol - 1))
-                def _():
-                    pass_on(hop, k, p, 1).wait_send()
-
-                @pl.when((p >= col) & (col > 0))
-                def _():
-                    pass_on(hop, k, p, 0).wait_send()
-            for i in range(1, nrow):
-                partial(hop, k, i).wait_send()
+            if k == CHUNKS - 1:
+                sent_all(functools.partial(spread, hop, k), ncol)
+            sent_all(functools.partial(partial, hop, k), nrow)
         swap(k).wait_send()
         for i in range(1, nrow):
             gw_rows(k, i).wait_send()
@@ -342,6 +309,11 @@
             gw_cols(k, i).wait_send()
             if split:
                 gw_share(k, i).wait_send()
+
+
+def emit(gf_in, gw_in, gf_ref, gw_ref):
+    gf_ref[...] = gf_in[...]
+    gw_ref[...] = gw_in[...].astype(F32)
 
 
 def per_device(
@@ -386,7 +358,7 @@
             pltpu.VMEM((slots + 1, side, side), BF16),
             pltpu.VMEM((half, side), BF16),
             pltpu.VMEM((2, CHUNKS, ncol, wide, side), BF16),
-            pltpu.VMEM((CHUNKS, nrow, wide, side), F32),
+            pltpu.VMEM((CHUNKS, wide, side), F32),
             pltpu.VMEM((2, CHUNKS, nrow, wide, side), BF16),
             pltpu.VMEM((2, CHUNKS, nrow, wide, side), BF16),
             pltpu.VMEM((CHUNKS, 2, side, wide), BF16),
@@ -396,7 +368,7 @@
             pltpu.VMEM((CHUNKS, held // piece, piece, 2 * wide), BF16),
             pltpu.VMEM((CHUNKS, nrow, held // piece, piece, 2 * wide), BF16),
             dma((8,)),
-            dma((2, CHUNKS, 2, ncol)), dma((2, CHUNKS, ncol)),
+            dma((2, CHUNKS, ncol)), dma((2, CHUNKS, ncol)),
             dma((2, CHUNKS, nrow)), dma((2, CHUNKS, nrow)),
             dma((CHUNKS,)), dma((CHUNKS,)),
             dma((CHUNKS, nrow)), dma((CHUNKS, nrow)),
@@ -409,7 +381,16 @@
     )(
         diffusion_time, node_features, weight, cotangent, tile_count.reshape(1),
         tile_row.reshape(slots), tile_col.reshape(slots), values)
-    return (grad_features, grad_weight.astype(F32))
+    return pl.pallas_call(
+        emit,
+        out_shape=(
+            jax.ShapeDtypeStruct((side, half), BF16),
+            jax.ShapeDtypeStruct((half, features), F32),
+        ),
+        in_specs=[vmem, vmem],
+        out_specs=(vmem, vmem),
+        compiler_params=pltpu.CompilerParams(vmem_limit_bytes=60 << 20),
+    )(grad_features, grad_weight)
 
 
 def solution(mesh):

time: 61.9 us -> 59.6 us (0.963)
  other arithmetic: 1.8 us -> 0 us
  local copies, waits for them, and re-layouts: 1.57 us -> 0 us
  Pallas kernels: 56.4 us -> 57.5 us
    pallas_call x0 -> x1, Pallas kernels: none -> 1.87 us  [per_device(): pl.pallas_call(emit, out_shape=(jax.ShapeDtypeStruct((side, half), BF16),...]
    convert_element_type x1 -> x0, other arithmetic: 1.8 us -> none  [per_device(): return (grad_features, grad_weight.astype(F32))]
    unnamed x1 -> x0, local copies, waits for them, and re-layouts: 1.57 us -> none
    pallas_call x1, Pallas kernels: 56.4 us -> 55.6 us  [per_device(): pl.pallas_call(functools.partial(hops, nrow, ncol, 1.0 / math.sqrt(side *...]
where the time goes in v3:
time: 59.6 us; the launch traced here: 59.4 us
  Pallas kernels  57.5 us (96%)
  between operations  1.93 us (3%)
    pallas_call x1, Pallas kernels, per_device(): pl.pallas_call(functools.partial(hops, nrow, ncol, 1.0 / math.sqrt(side *...  55.6 us
    pallas_call x1, Pallas kernels, per_device(): pl.pallas_call(emit, out_shape=(jax.ShapeDtypeStruct((side, half), BF16),...  1.87 us

profile of v3, /device:TPU:0, one launch (start us, length us, event | category | flops | bytes accessed | tf_op | source)
XLA Modules:
  0.0 59.4 jit_solution(12718437497337092184)
XLA Ops:
  1.9 55.6 %shard_map.95 = (bf16[256,256]{1,0:T(8,128)(2,1)}, bf16[256,512]{1,0:T(8,128)(2,1)}) custom-call(f32[1]{0:T(128)S(6)} %copy.10.t_hbm, bf16[256,256]{1,0:T(8,128)(2,1)} %x_hbm.1, bf16[256,512]{1,0:T(8,128)(2,1)} %w_hbm.1, bf16[256,256]{1,0:T(8,128)(2,1)} %g_hbm.1, s32[1]{0:T(128)} %bitcast.4.count_hbm, s32[24]{0:T(128)} %bitcast.6, s32[24]{0:T(128)} %bitcast.7, ...), custom_call_target="tpu_custom_call" | custom-call | tf_op jit(solution)/shard_map/pallas_call | solution.py:335
  57.5 1.9 %shard_map.96 = (bf16[256,256]{1,0:T(8,128)(2,1)}, f32[256,512]{1,0:T(8,128)}) custom-call(bf16[256,256]{1,0:T(8,128)(2,1)} %get-tuple-element.4.gf_in, bf16[256,512]{1,0:T(8,128)(2,1)} %get-tuple-element.5.gw_in), custom_call_target="tpu_custom_call" | custom-call | tf_op jit(solution)/shard_map/pallas_call | solution.py:384

commit v4 on v3

--- a/solution.py
+++ b/solution.py
@@ -96,7 +96,7 @@
         return to_row(piece, piece, w3_s.at[k, i], w3_r.at[k, i], i)
 
     def start_all(copy, n):
-        for i in range(1, n):
+        for i in sorted(range(1, n), key=lambda i: -abs(2 * i - n)):
             copy(i).start()
 
     def recv_all(copy, n):
@@ -331,7 +331,7 @@
     dma = pltpu.SemaphoreType.DMA
     hbm = pl.BlockSpec(memory_space=pltpu.HBM)
     held = half // nrow
-    piece = held // ncol if (held // ncol) % 16 == 0 else held
+    piece = held
     grad_features, grad_weight = pl.pallas_call(
         functools.partial(hops, nrow, ncol, 1.0 / math.sqrt(side * places)),
         out_shape=(

time: 59.6 us -> 56.2 us (0.943)
  Pallas kernels: 57.5 us -> 54.1 us
    pallas_call x1, Pallas kernels: 55.6 us -> 52.2 us  [per_device(): pl.pallas_call(functools.partial(hops, nrow, ncol, 1.0 / math.sqrt(side *...]
where the time goes in v4:
time: 56.2 us; the launch traced here: 56 us
  Pallas kernels  54.1 us (96%)
  between operations  1.93 us (3%)
    pallas_call x1, Pallas kernels, per_device(): pl.pallas_call(functools.partial(hops, nrow, ncol, 1.0 / math.sqrt(side *...  52.2 us
    pallas_call x1, Pallas kernels, per_device(): pl.pallas_call(emit, out_shape=(jax.ShapeDtypeStruct((side, half), BF16),...  1.87 us

profile of v4, /device:TPU:0, one launch (start us, length us, event | category | flops | bytes accessed | tf_op | source)
XLA Modules:
  0.0 56.0 jit_solution(8939563053864629096)
XLA Ops:
  1.9 52.2 %shard_map.95 = (bf16[256,256]{1,0:T(8,128)(2,1)}, bf16[256,512]{1,0:T(8,128)(2,1)}) custom-call(f32[1]{0:T(128)S(6)} %copy.10.t_hbm, bf16[256,256]{1,0:T(8,128)(2,1)} %x_hbm.1, bf16[256,512]{1,0:T(8,128)(2,1)} %w_hbm.1, bf16[256,256]{1,0:T(8,128)(2,1)} %g_hbm.1, s32[1]{0:T(128)} %bitcast.4.count_hbm, s32[24]{0:T(128)} %bitcast.6, s32[24]{0:T(128)} %bitcast.7, ...), custom_call_target="tpu_custom_call" | custom-call | tf_op jit(solution)/shard_map/pallas_call | solution.py:335
  54.1 1.9 %shard_map.96 = (bf16[256,256]{1,0:T(8,128)(2,1)}, f32[256,512]{1,0:T(8,128)}) custom-call(bf16[256,256]{1,0:T(8,128)(2,1)} %get-tuple-element.4.gf_in, bf16[256,512]{1,0:T(8,128)(2,1)} %get-tuple-element.5.gw_in), custom_call_target="tpu_custom_call" | custom-call | tf_op jit(solution)/shard_map/pallas_call | solution.py:384
